TPU v7x, 256 devices: a whole 4x4x8 slice. The times are simulated.
256 devices in a mesh: dp: 8 (over z_hi, y), proto: 32 (over z_lo, x, core).
Axes of the slice: x: 4, y: 4, z: 8 (z_hi: 2, z_lo: 4; z = z_hi * 4 + z_lo), core: 2. Of those that a mesh axis runs over, the one named last changes fastest.
Arguments:
- teacher_global: bfloat16 [1024, 2, 256], P(('dp', 'proto')), may hold values from -700 to 700
- queue: bfloat16 [3072, 256], P(('dp', 'proto')), may hold values from -700 to 700
- student: bfloat16 [1024, 10, 256], P(('dp', 'proto')), may hold values from -700 to 700
- prototypes: bfloat16 [131072, 256], P('proto'), may hold values from -700 to 700
Outputs:
- student_grad: float32 [1024, 10, 256], P(('dp', 'proto'))
- crop_loss: float32 [1024, 10], P(('dp', 'proto'))
All inputs are finite; a program needn't handle non-finite values.
Results may differ from a plain program's by a relative error of at most 0.004.
Values may be sent and summed in bfloat16 or wider, within the bound.
No kernel may reach another device: no remote copies, remote signals or barrier semaphores. Data moves between devices by JAX's collectives and lax.ppermute only.
A program may use at most 128 MiB of HBM per device.

v0:
```python
import functools
import math

import jax
import jax.numpy as jnp
from jax import lax
from jax.experimental import pallas as pl
from jax.experimental.pallas import tpu as pltpu
from jax.sharding import PartitionSpec as P

SINK_ITERS = 3
TEACHER_SOFTNESS = 0.07
STUDENT_SOFTNESS = 0.1
NORM_EPSILON = 1e-06
TEACHER_EXP2 = math.log2(math.e) / TEACHER_SOFTNESS
STUDENT_EXP2 = math.log2(math.e) / STUDENT_SOFTNESS

LANES = 128
MIB = 1024 * 1024

f32 = jnp.float32
bf16 = jnp.bfloat16
shape = jax.ShapeDtypeStruct


def iota(shape, dim):
    return lax.broadcasted_iota(jnp.int32, shape, dim)


def unit(values):
    return values * lax.rsqrt(jnp.sum(values * values, axis=-1, keepdims=True) + NORM_EPSILON)


def nt_dot(a, b):
    return lax.dot_general(a, b, (((1,), (1,)), ((), ())), preferred_element_type=f32)


def call(kernel, name, out_shape, flops=0, nbytes=0, exps=0, vmem=16, **kw):
    return pl.pallas_call(
        kernel,
        out_shape=out_shape,
        compiler_params=pltpu.CompilerParams(vmem_limit_bytes=vmem * MIB),
        cost_estimate=pl.CostEstimate(flops=flops, bytes_accessed=nbytes, transcendentals=exps),
        name=name,
        **kw,
    )


def in_vmem(array):
    return pltpu.with_memory_space_constraint(array, pltpu.VMEM)


def in_hbm(array):
    return pltpu.with_memory_space_constraint(array, pltpu.HBM)


def pack_kernel(student_ref, teacher_ref, queue_ref, out_ref, rows_ref):
    crops, images, width = student_ref.shape
    stud, glob = crops * images, 2 * images
    half = width // 2

    def put(at, rows, height, values):
        rows_ref[at + rows : at + rows + values.shape[0], :] = values[:, :half]
        rows_ref[at + height + rows : at + height + rows + values.shape[0], :] = values[:, half:]

    for c in range(crops):
        put(0, c * images, stud, unit(student_ref[c].astype(f32)))
    at = 2 * stud
    for i in range(images):
        views = unit(teacher_ref[i].astype(f32))
        put(at, i, glob, views[1:2])
        put(at, images + i, glob, views[0:1])
    units = unit(queue_ref[...].astype(f32))
    at = at + 2 * glob
    put(at, 0, 8, units[:8])
    put(at + 16, 0, 4, units[8:])
    packed = rows_ref[...].astype(bf16)
    for j in range(out_ref.shape[0]):
        out_ref[j] = packed


def wide(low, high):
    return jnp.concatenate([low, high], axis=-1)


def unit_kernel(protos_ref, out_ref, raw_ref, sems):
    parts = sems.shape[0]
    rows = raw_ref.shape[0] // parts
    copies = []
    for j in range(parts):
        here = pl.ds(j * rows, rows)
        copies.append(pltpu.make_async_copy(protos_ref.at[here], raw_ref.at[here], sems.at[j]))
        copies[j].start()
    for j in range(parts):
        copies[j].wait()
        here = slice(j * rows, (j + 1) * rows)
        out_ref[here, :] = unit(raw_ref[here, :].astype(f32)).astype(bf16)


def by_core(core_ref, own, other):
    is_first = core_ref[0] == 0
    return jnp.where(is_first, own, other), jnp.where(is_first, other, own)


def teacher_kernel(stud, glob, core_ref, own_ref, other_ref, unit_ref, exp_ref, sums_ref):
    chips, _, half = own_ref.shape
    width = 2 * half
    at = 2 * stud
    blocks = by_core(core_ref, own_ref[...].astype(f32)[:, at:], other_ref[...].astype(f32)[:, at:])
    block = jnp.concatenate(blocks, axis=0)
    groups = 2 * chips
    at = 2 * glob
    g = wide(block[:, :glob], block[:, glob:at]).reshape(groups * glob, width)
    q = wide(block[:, at : at + 8], block[:, at + 8 : at + 16]).reshape(groups * 8, width)
    r = block[:, at + 16 :].reshape(chips, 2, 8, half)
    turned = jnp.concatenate([r[:, :, 4:], r[:, :, :4]], axis=2)
    top = iota((chips, 8, half), 1) < 4
    r = wide(jnp.where(top, r[:, 0], turned[:, 1]), jnp.where(top, turned[:, 0], r[:, 1]))
    r = r.reshape(groups * 4, width)
    teach = jnp.concatenate([g, q, r], axis=0).astype(bf16)
    step = 256
    for start in range(0, unit_ref.shape[0], step):
        here = slice(start, start + step)
        exps = jnp.exp2(nt_dot(teach, unit_ref[here, :]) * TEACHER_EXP2)
        exp_ref[:, here] = exps.astype(bf16)
        sums = jnp.sum(exps, axis=0, keepdims=True)
        for k in range(step // LANES):
            at = start // LANES + k
            sums_ref[at : at + 1, :] = sums[:, k * LANES : (k + 1) * LANES]


def other_core_kernel(stud, glob, own_ref, unit_ref, exp_ref):
    chips, _, half = own_ref.shape
    at = 2 * stud
    block = own_ref[...].astype(f32)[:, at : at + 2 * glob]
    teach = wide(block[:, :glob], block[:, glob:]).reshape(chips * glob, 2 * half).astype(bf16)
    step = 512
    for start in range(0, unit_ref.shape[0], step):
        here = slice(start, start + step)
        exp_ref[:, here] = jnp.exp2(nt_dot(teach, unit_ref[here, :]) * TEACHER_EXP2).astype(bf16)


def add_students(stud, own_ref, unit_ref, stud_ref, acc_ref, tot_ref, start_acc, start_tot):
    chips, _, half = own_ref.shape
    block = own_ref[...].astype(f32)[:, : 2 * stud]
    block = wide(block[:, :stud], block[:, stud:])
    stud_ref[...] = block.reshape(chips * stud, 2 * half).astype(bf16)
    step = 512
    for start in range(0, unit_ref.shape[0], step):
        protos = unit_ref[start : start + step, :]
        weights = jnp.exp2(nt_dot(stud_ref[...], protos) * STUDENT_EXP2)
        part = weights[:, :LANES]
        for k in range(1, step // LANES):
            part = part + weights[:, k * LANES : (k + 1) * LANES]
        term = jnp.dot(weights.astype(bf16), protos, preferred_element_type=f32)
        if start == 0 and start_acc is None:
            tot_ref[...] = part
            acc_ref[...] = term
        elif start == 0:
            tot_ref[...] = start_tot[...] + part
            acc_ref[...] = start_acc[...] + term
        else:
            tot_ref[...] += part
            acc_ref[...] += term


def student_own_kernel(stud, own_ref, unit_ref, acc_ref, tot_ref, stud_ref):
    add_students(stud, own_ref, unit_ref, stud_ref, acc_ref, tot_ref, None, None)


def student_other_kernel(
    stud, own_ref, unit_ref, start_acc, start_tot, attract_ref, total_ref, stud_ref, acc_ref, tot_ref
):
    add_students(stud, own_ref, unit_ref, stud_ref, acc_ref, tot_ref, start_acc, start_tot)
    chips = own_ref.shape[0]
    attract = acc_ref[...].reshape(chips, stud, 2 * LANES)
    attract = jnp.concatenate([attract[:, :, :LANES], attract[:, :, LANES:]], axis=1)
    attract_ref[...] = attract.astype(bf16)
    total = jnp.sum(tot_ref[...], axis=1, keepdims=True).reshape(chips, stud, 1)
    eye = iota((chips, stud, LANES), 1) == iota((chips, stud, LANES), 2)
    total_ref[...] = jnp.sum(
        jnp.where(eye, jnp.broadcast_to(total, (chips, stud, LANES)), 0.0), axis=1, keepdims=True
    )


def pair_kernel(mine_ref, got_ref, out_ref):
    total = mine_ref[...] + got_ref[...]
    for j in range(out_ref.shape[0]):
        out_ref[j] = total


def proto_scale_of(parts_ref):
    total = parts_ref[0].astype(f32)
    for j in range(1, parts_ref.shape[0]):
        total = total + parts_ref[j].astype(f32)
    scale = 1.0 / total
    return jnp.concatenate([scale[k : k + 1, :] for k in range(scale.shape[0])], axis=1)


def col_kernel(parts_ref, exp_ref, out_ref):
    scale = proto_scale_of(parts_ref)
    rows, cols = exp_ref.shape
    lines = []
    for g in range(rows // LANES):
        acc = None
        for k in range(cols // LANES):
            lanes = slice(k * LANES, (k + 1) * LANES)
            term = exp_ref[g * LANES : (g + 1) * LANES, lanes].astype(f32) * scale[:, lanes]
            acc = term if acc is None else acc + term
        lines.append(jnp.sum(acc.T, axis=0, keepdims=True))
    out = jnp.concatenate(lines, axis=1)
    for j in range(out_ref.shape[0]):
        out_ref[j] = out


def row_kernel(parts_ref, exp_ref, out_ref, line_ref):
    rows, cols = exp_ref.shape
    scale = 1.0 / jnp.sum(parts_ref[...], axis=0)
    acc = None
    for g in range(rows // LANES):
        tall = jnp.broadcast_to(scale[:, g * LANES : (g + 1) * LANES], (LANES, LANES)).T
        for t in range(0, LANES, 16):
            scales = jnp.concatenate([tall[t : t + 16]] * (cols // LANES), axis=1)
            term = exp_ref[g * LANES + t : g * LANES + t + 16, :].astype(f32) * scales
            term = term[:8] + term[8:]
            acc = term if acc is None else acc + term
    line = jnp.sum(acc, axis=0, keepdims=True)
    for k in range(cols // LANES):
        line_ref[k : k + 1, :] = line[:, k * LANES : (k + 1) * LANES]
    sums = line_ref[...].astype(bf16)
    for j in range(out_ref.shape[0]):
        out_ref[j] = sums


def add_repel(parts_ref, exps_of, unit_ref, repel, mass):
    scale = proto_scale_of(parts_ref)
    step = 512
    for start in range(0, unit_ref.shape[0], step):
        here = slice(start, start + step)
        terms = exps_of(here).astype(f32) * scale[:, here]
        for k in range(step // LANES):
            mass = mass + terms[:, k * LANES : (k + 1) * LANES]
        repel = repel + jnp.dot(terms.astype(bf16), unit_ref[here, :], preferred_element_type=f32)
    return repel, mass


def repel_own_kernel(core_ref, parts_ref, exp_ref, unit_ref, repel_ref, mass_ref):
    rows = repel_ref.shape[0]
    mine = pl.ds(pl.multiple_of(core_ref[0] * rows, rows), rows)
    repel_ref[...], mass_ref[...] = add_repel(
        parts_ref,
        lambda here: exp_ref[mine, here],
        unit_ref,
        jnp.zeros(repel_ref.shape, f32),
        jnp.zeros(mass_ref.shape, f32),
    )


def repel_other_kernel(
    stud, parts_ref, exp_ref, unit_ref, repel_ref, mass_ref, attract_ref, total_ref, out_ref
):
    repel, mass = add_repel(
        parts_ref, lambda here: exp_ref[:, here], unit_ref, repel_ref[...], mass_ref[...]
    )
    chips = attract_ref.shape[0]
    glob = repel.shape[0] // chips
    repel = repel.reshape(chips, glob, 2 * LANES)
    dims = (chips, glob, LANES)
    place = iota(dims, 1) + stud == iota(dims, 2)
    mass = jnp.sum(mass, axis=1, keepdims=True).reshape(chips, glob, 1)
    mass = jnp.where(place, jnp.broadcast_to(mass, dims), 0.0)
    scalars = total_ref[...] + jnp.sum(mass, axis=1, keepdims=True)
    high = scalars.astype(bf16).astype(f32)
    scalars = jnp.where(iota(dims, 1) == 0, high, scalars - high)
    parts = [attract_ref[...].astype(f32), repel[:, :, :LANES], repel[:, :, LANES:], scalars]
    out_ref[...] = jnp.concatenate(parts, axis=1).astype(bf16)


def final_kernel(back_ref, student_ref, grad_ref, loss_ref, rows_ref):
    crops, images, width = student_ref.shape
    stud = crops * images
    for c in range(crops):
        rows_ref[c * images : (c + 1) * images, :] = student_ref[c].astype(f32)
    values = rows_ref[...]
    back = jnp.sum(back_ref[...].astype(f32), axis=0)
    attract = wide(back[:stud], back[stud : 2 * stud])
    back = back[2 * stud :]
    line = back[16:17] + back[17:18]
    sub, lane = iota((stud, LANES), 0), iota((stud, LANES), 1)
    lines = jnp.broadcast_to(line, (stud, LANES))
    total = jnp.sum(jnp.where(lane == sub, lines, 0.0), axis=1, keepdims=True)
    mass = jnp.sum(jnp.where(lane == sub + stud, lines, 0.0)[:8], axis=1, keepdims=True)
    views = wide(back[:8], back[8:16]) / mass
    both = views + jnp.concatenate([views[images:], views[:images]], axis=0)
    repel = jnp.concatenate([views] + [both] * (stud // 8 - 1), axis=0)
    pairs = jnp.where(iota((stud, 1), 0) < 2 * images, 1.0, 2.0)
    inv_norm = lax.rsqrt(jnp.sum(values * values, axis=1, keepdims=True) + NORM_EPSILON)
    own = values * inv_norm
    low = own.astype(bf16).astype(f32)
    grad_unit = (pairs * attract / total - repel) / STUDENT_SOFTNESS
    cross = jnp.sum(low * repel, axis=1, keepdims=True) / STUDENT_SOFTNESS
    loss = pairs * jnp.log(total) - cross
    inner = jnp.sum(own * grad_unit, axis=1, keepdims=True)
    grad = inv_norm * (grad_unit - own * inner)
    for c in range(crops):
        grad_ref[c] = grad[c * images : (c + 1) * images]
    spreads = jnp.broadcast_to(loss, (stud, LANES))
    for i in range(images):
        spread = jnp.where(sub == lane * images + i, spreads, 0.0)
        loss_ref[i : i + 1, :] = jnp.sum(spread, axis=0, keepdims=True)[:, :crops]


def exchange(array, axis, **kw):
    return lax.all_to_all(array, axis, 0, 0, tiled=True, **kw)


def body(teacher_global, queue, student, prototypes):
    images, crops, width = student.shape
    queue_rows = queue.shape[0]
    groups, parts = lax.axis_size("proto"), lax.axis_size("dp")
    chips = groups // 2
    stud, glob = images * crops, images * 2
    teach_rows = groups * (glob + queue_rows)
    protos = prototypes.shape[0]
    student = jnp.transpose(student, (1, 0, 2))
    core = jnp.reshape(lax.axis_index("proto") & 1, (1,))
    core, student = lax.optimization_barrier((core, student))
    scalar = pl.BlockSpec(memory_space=pltpu.SMEM)
    vmem = pl.BlockSpec(memory_space=pltpu.VMEM)

    def swap(array):
        return lax.ppermute(array, "proto", [(j, j ^ 1) for j in range(groups)])

    send_rows = 2 * (stud + glob + queue_rows)
    packed = call(
        pack_kernel,
        "pack_rows",
        shape((chips, send_rows, LANES), bf16),
        scratch_shapes=[pltpu.VMEM((send_rows, LANES), f32)],
    )(*map(in_hbm, (student, teacher_global, queue)))
    same_core = [list(range(c, groups, 2)) for c in range(2)]
    own_rows = exchange(packed, "proto", axis_index_groups=same_core)
    other_rows = swap(own_rows)
    own_rows, prototypes = lax.optimization_barrier((own_rows, prototypes))
    unit_protos = call(
        unit_kernel,
        "unit_prototypes",
        shape((protos, width), bf16),
        in_specs=[pl.BlockSpec(memory_space=pl.ANY)],
        scratch_shapes=[pltpu.VMEM((protos, width), bf16), pltpu.SemaphoreType.DMA((8,))],
        flops=3 * protos * width,
        nbytes=4 * protos * width,
    )(in_hbm(prototypes))

    other_rows, unit_protos = lax.optimization_barrier((other_rows, unit_protos))
    other_protos = swap(unit_protos)
    exps, row_parts = call(
        functools.partial(teacher_kernel, stud, glob),
        "teacher_exponentials",
        [pltpu.VMEM((teach_rows, protos), bf16), shape((protos // LANES, LANES), f32)],
        in_specs=[scalar, vmem, vmem, vmem],
        flops=2 * teach_rows * protos * width,
        nbytes=2 * teach_rows * protos,
        exps=teach_rows * protos,
    )(core, own_rows, other_rows, unit_protos)
    exps = in_vmem(exps)

    row_parts, own_rows = lax.optimization_barrier((row_parts, own_rows))
    half = parts // 2
    got_sums = lax.ppermute(row_parts, "dp", [(j, (j + half) % parts) for j in range(parts)])
    own_students = chips * stud
    work = dict(
        flops=4 * own_students * protos * width,
        nbytes=2 * protos * width,
        exps=own_students * protos,
    )
    rows_scratch = pltpu.VMEM((own_students, width), bf16)
    acc, tot = call(
        functools.partial(student_own_kernel, stud),
        "students_own_core",
        [shape((own_students, width), f32), shape((own_students, LANES), f32)],
        scratch_shapes=[rows_scratch],
        **work,
    )(own_rows, unit_protos)
    attract, total = call(
        functools.partial(student_other_kernel, stud),
        "students_other_core",
        [shape((chips, 2 * stud, LANES), bf16), shape((chips, 1, LANES), f32)],
        scratch_shapes=[
            rows_scratch,
            pltpu.VMEM((own_students, width), f32),
            pltpu.VMEM((own_students, LANES), f32),
        ],
        **work,
    )(own_rows, other_protos, acc, tot)
    own_glob = chips * glob
    other_exps = call(
        functools.partial(other_core_kernel, stud, glob),
        "teacher_other_core",
        pltpu.VMEM((own_glob, protos), bf16),
        flops=2 * own_glob * protos * width,
        nbytes=2 * protos * width,
        exps=own_glob * protos,
    )(own_rows, other_protos)
    got_sums, attract, total, other_exps = lax.optimization_barrier(
        (got_sums, attract, total, other_exps)
    )
    other_exps = in_vmem(other_exps)
    row_parts = call(pair_kernel, "add_halves", shape((half, protos // LANES, LANES), f32))(row_parts, got_sums)
    halves = [list(range(half)), list(range(half, parts))]
    row_parts = exchange(row_parts, "dp", axis_index_groups=halves)

    for iteration in range(SINK_ITERS - 1):
        col_parts = call(
            col_kernel,
            "sum_over_prototypes",
            shape((groups, 1, teach_rows), f32),
            flops=2 * teach_rows * protos,
            nbytes=2 * teach_rows * protos,
        )(row_parts, exps)
        col_parts = exchange(col_parts, "proto")
        row_parts = call(
            row_kernel,
            "sum_over_rows",
            shape((parts, protos // LANES, LANES), bf16),
            scratch_shapes=[pltpu.VMEM((protos // LANES, LANES), f32)],
            flops=2 * teach_rows * protos,
            nbytes=2 * teach_rows * protos,
        )(col_parts, exps)
        row_parts = exchange(row_parts, "dp")

    other_parts = swap(row_parts)
    work = dict(flops=2 * own_glob * protos * width, nbytes=4 * protos * width)
    repel, mass = call(
        repel_own_kernel,
        "repel_own_core",
        [shape((own_glob, width), f32), shape((own_glob, LANES), f32)],
        in_specs=[scalar] + [vmem] * 3,
        **work,
    )(core, row_parts, exps, unit_protos)
    back = call(
        functools.partial(repel_other_kernel, stud),
        "repel_other_core",
        shape((chips, 2 * stud + 2 * glob + 8, LANES), bf16),
        **work,
    )(other_parts, other_exps, other_protos, repel, mass, attract, total)
    back = exchange(back, "proto", axis_index_groups=same_core)

    grad, loss = call(
        final_kernel,
        "gradients",
        [shape((crops, images, width), f32), shape((images, crops), f32)],
        scratch_shapes=[pltpu.VMEM((stud, width), f32)],
    )(back, student)
    return jnp.transpose(grad, (1, 0, 2)), loss


def solution(mesh):
    in_specs = (
        P(("dp", "proto"), None, None),
        P(("dp", "proto"), None),
        P(("dp", "proto"), None, None),
        P("proto", None),
    )
    out_specs = (P(("dp", "proto"), None, None), P(("dp", "proto"), None))
    return jax.shard_map(body, mesh=mesh, in_specs=in_specs, out_specs=out_specs, check_vma=False)
```

profile of v0, /device:TPU:1, one launch (start us, length us, event | category | flops | bytes accessed | tf_op | source)
XLA Modules:
  0.0 124.3 jit_solution(2915685017865770758)
XLA Ops:
  0.6 0.9 pack_rows.1
  1.5 22.1 %all_to_all.35.own_ref = bf16[16,120,128]{2,1,0:T(8,128)(2,1)S(1)} all-to-all(bf16[16,120,128]{2,1,0:T(8,128)(2,1)S(1)} %pack_rows.1), channel_id=1, replica_groups={{0,2,4,6,8,10,12,14,16,18,20,22,24,26,28,30},{1,3,5,7,9,11,13,15,17,19,..., dimensions={0} | all-to-all | bytes 983040 | tf_op jit(solution)/shard_map/all_to_all | solution.py:314
  23.6 2.5 %collective-permute-start = (bf16[16,120,128]{2,1,0:T(8,128)(2,1)S(1)}, bf16[16,120,128]{2,1,0:T(8,128)(2,1)S(1)}, u32[]{:S(2)}, u32[]{:S(2)}) collective-permute-start(bf16[16,120,128]{2,1,0:T(8,128)(2,1)S(1)} %all_to_all.35.own_ref), channel_id=1, source_target_pairs={{0,1},{1,0},{2,3},{3,2},{4,5},{5,4},{6,7},{7,6},{8,9},{9,8},{10,11... | collective-permute-start | bytes 1474568 | tf_op jit(solution)/shard_map/ppermute | solution.py:332
  26.1 2.3 %unit_prototypes.1.unit_ref = bf16[4096,256]{1,0:T(8,128)(2,1)S(1)} custom-call(bf16[4096,256]{1,0:T(8,128)(2,1)} %protos_ref), custom_call_target="tpu_custom_call" | custom-call | flops 3145728 | bytes 4194304 | tf_op jit(solution)/shard_map/unit_prototypes/pallas_call | solution.py:345
  28.4 0.0 collective-permute-done.other_ref
  28.4 0.1 collective-permute-start.2
  28.5 1.6 %teacher_exponentials.1 = (bf16[640,4096]{1,0:T(8,128)(2,1)S(1)}, f32[32,128]{1,0:T(8,128)S(1)}) custom-call(s32[1]{0:T(128)} %bitcast.core_ref, bf16[16,120,128]{2,1,0:T(8,128)(2,1)S(1)} %all_to_all.35.own_ref, bf16[16,120,128]{2,1,0:T(8,128)(2,1)S(1)} %collective-permute-done.other_ref, bf16[4096,256]{1,0:T(8,128)(2,1)S(1)} %unit_prototypes.1.unit_ref), custom_call_target="tpu_custom_call" | custom-call | flops 1342177280 | bytes 5242880 | tf_op jit(solution)/shard_map/teacher_exponentials/pallas_call | solution.py:357
  30.1 4.3 %collective-permute-start.1 = (f32[32,128]{1,0:T(8,128)S(1)}, f32[32,128]{1,0:T(8,128)S(1)}, u32[]{:S(2)}, u32[]{:S(2)}) collective-permute-start(f32[32,128]{1,0:T(8,128)S(1)} %get-tuple-element.31.mine_ref), channel_id=1, source_target_pairs={{0,128},{32,160},{64,192},{96,224},{128,0},{160,32},{192,64},{224,... | collective-permute-start | bytes 49160 | tf_op jit(solution)/shard_map/ppermute | solution.py:370
  34.4 3.1 %students_own_core.1 = (f32[640,256]{1,0:T(8,128)S(1)}, f32[640,128]{1,0:T(8,128)S(1)}) custom-call(bf16[16,120,128]{2,1,0:T(8,128)(2,1)S(1)} %all_to_all.35.own_ref, bf16[4096,256]{1,0:T(8,128)(2,1)S(1)} %unit_prototypes.1.unit_ref), custom_call_target="tpu_custom_call" | custom-call | flops 2684354560 | bytes 2097152 | tf_op jit(solution)/shard_map/students_own_core/pallas_call | solution.py:378
  37.5 0.0 collective-permute-done.2.unit_ref
  37.5 3.1 %students_other_core.1 = (bf16[16,80,128]{2,1,0:T(8,128)(2,1)S(1)}, f32[16,1,128]{2,1,0:T(1,128)S(1)}) custom-call(bf16[16,120,128]{2,1,0:T(8,128)(2,1)S(1)} %all_to_all.35.own_ref, bf16[4096,256]{1,0:T(8,128)(2,1)S(1)} %collective-permute-done.2.unit_ref, f32[640,256]{1,0:T(8,128)S(1)} %get-tuple-element.33.start_acc, ...), custom_call_target="tpu_custom_call" | custom-call | flops 2684354560 | bytes 2097152 | tf_op jit(solution)/shard_map/students_other_core/pallas_call | solution.py:385
  40.6 0.8 teacher_other_core.1.exp_ref
  41.4 0.0 collective-permute-done.1.got_ref
  41.5 8.5 %all_to_all.36.parts_ref = f32[4,32,128]{2,1,0:T(8,128)S(1)} all-to-all(f32[4,32,128]{2,1,0:T(8,128)S(1)} %add_halves.1), channel_id=1, replica_groups={{0,32,64,96},{128,160,192,224},{1,33,65,97},{129,161,193,225},{2,34,66,..., dimensions={0} | all-to-all | bytes 131072 | tf_op jit(solution)/shard_map/all_to_all | solution.py:314
  49.9 1.1 sum_over_prototypes.2
  51.1 14.3 %all_to_all.37.parts_ref = f32[32,1,640]{2,1,0:T(1,128)S(1)} all-to-all(f32[32,1,640]{2,1,0:T(1,128)S(1)} %sum_over_prototypes.2), channel_id=1, replica_groups=mesh['dp'=8,'proto'=32] {'proto'}, dimensions={0} | all-to-all | bytes 163840 | tf_op jit(solution)/shard_map/all_to_all | solution.py:314
  65.4 1.3 %sum_over_rows.2 = bf16[8,32,128]{2,1,0:T(8,128)(2,1)S(1)} custom-call(f32[32,1,640]{2,1,0:T(1,128)S(1)} %all_to_all.37.parts_ref, bf16[640,4096]{1,0:T(8,128)(2,1)S(1)} %get-tuple-element.38.exp_ref), custom_call_target="tpu_custom_call" | custom-call | flops 5242880 | bytes 5242880 | tf_op jit(solution)/shard_map/sum_over_rows/pallas_call | solution.py:422
  66.7 11.9 %all_to_all.38.parts_ref = bf16[8,32,128]{2,1,0:T(8,128)(2,1)S(1)} all-to-all(bf16[8,32,128]{2,1,0:T(8,128)(2,1)S(1)} %sum_over_rows.2), channel_id=1, replica_groups=mesh['dp'=8,'proto'=32] {'dp'}, dimensions={0} | all-to-all | bytes 131072 | tf_op jit(solution)/shard_map/all_to_all | solution.py:314
  78.7 1.1 sum_over_prototypes.3
  79.8 12.7 %all_to_all.39.parts_ref = f32[32,1,640]{2,1,0:T(1,128)S(1)} all-to-all(f32[32,1,640]{2,1,0:T(1,128)S(1)} %sum_over_prototypes.3), channel_id=1, replica_groups=mesh['dp'=8,'proto'=32] {'proto'}, dimensions={0} | all-to-all | bytes 163840 | tf_op jit(solution)/shard_map/all_to_all | solution.py:314
  92.5 1.3 %sum_over_rows.3 = bf16[8,32,128]{2,1,0:T(8,128)(2,1)S(1)} custom-call(f32[32,1,640]{2,1,0:T(1,128)S(1)} %all_to_all.39.parts_ref, bf16[640,4096]{1,0:T(8,128)(2,1)S(1)} %get-tuple-element.38.exp_ref), custom_call_target="tpu_custom_call" | custom-call | flops 5242880 | bytes 5242880 | tf_op jit(solution)/shard_map/sum_over_rows/pallas_call | solution.py:422
  93.8 11.5 %all_to_all.40.parts_ref = bf16[8,32,128]{2,1,0:T(8,128)(2,1)S(1)} all-to-all(bf16[8,32,128]{2,1,0:T(8,128)(2,1)S(1)} %sum_over_rows.3), channel_id=1, replica_groups=mesh['dp'=8,'proto'=32] {'dp'}, dimensions={0} | all-to-all | bytes 131072 | tf_op jit(solution)/shard_map/all_to_all | solution.py:314
  105.3 1.6 %collective-permute-start.3 = (bf16[8,32,128]{2,1,0:T(8,128)(2,1)S(1)}, bf16[8,32,128]{2,1,0:T(8,128)(2,1)S(1)}, u32[]{:S(2)}, u32[]{:S(2)}) collective-permute-start(bf16[8,32,128]{2,1,0:T(8,128)(2,1)S(1)} %all_to_all.40.parts_ref), channel_id=1, source_target_pairs={{0,1},{1,0},{2,3},{3,2},{4,5},{5,4},{6,7},{7,6},{8,9},{9,8},{10,11... | collective-permute-start | bytes 196616 | tf_op jit(solution)/shard_map/ppermute | solution.py:332
  106.9 0.6 repel_own_core.1
  107.5 0.3 collective-permute-done.3.parts_ref
  107.8 0.0 copy-start
  107.8 0.6 repel_other_core.1
  108.4 15.1 %all_to_all.41.back_ref = bf16[16,104,128]{2,1,0:T(8,128)(2,1)S(1)} all-to-all(bf16[16,104,128]{2,1,0:T(8,128)(2,1)S(1)} %repel_other_core.1), channel_id=1, replica_groups={{0,2,4,6,8,10,12,14,16,18,20,22,24,26,28,30},{1,3,5,7,9,11,13,15,17,19,..., dimensions={0} | all-to-all | bytes 851968 | tf_op jit(solution)/shard_map/all_to_all | solution.py:314
  123.5 0.0 copy-done
  123.5 0.8 gradients.1
  (1 shorter events, 0.0 us)
Async XLA Ops:
  23.6 4.8 %collective-permute-start = (bf16[16,120,128]{2,1,0:T(8,128)(2,1)S(1)}, bf16[16,120,128]{2,1,0:T(8,128)(2,1)S(1)}, u32[]{:S(2)}, u32[]{:S(2)}) collective-permute-start(bf16[16,120,128]{2,1,0:T(8,128)(2,1)S(1)} %all_to_all.35.own_ref), channel_id=1, source_target_pairs={{0,1},{1,0},{2,3},{3,2},{4,5},{5,4},{6,7},{7,6},{8,9},{9,8},{10,11... | collective-permute-start | bytes 1474568 | tf_op jit(solution)/shard_map/ppermute | solution.py:332
  28.4 9.1 %collective-permute-start.2 = (bf16[4096,256]{1,0:T(8,128)(2,1)S(1)}, bf16[4096,256]{1,0:T(8,128)(2,1)S(1)}, u32[]{:S(2)}, u32[]{:S(2)}) collective-permute-start(bf16[4096,256]{1,0:T(8,128)(2,1)S(1)} %unit_prototypes.1.unit_ref), channel_id=1, source_target_pairs={{0,1},{1,0},{2,3},{3,2},{4,5},{5,4},{6,7},{7,6},{8,9},{9,8},{10,11... | collective-permute-start | bytes 6291464 | tf_op jit(solution)/shard_map/ppermute | solution.py:332
  30.1 11.3 %collective-permute-start.1 = (f32[32,128]{1,0:T(8,128)S(1)}, f32[32,128]{1,0:T(8,128)S(1)}, u32[]{:S(2)}, u32[]{:S(2)}) collective-permute-start(f32[32,128]{1,0:T(8,128)S(1)} %get-tuple-element.31.mine_ref), channel_id=1, source_target_pairs={{0,128},{32,160},{64,192},{96,224},{128,0},{160,32},{192,64},{224,... | collective-permute-start | bytes 49160 | tf_op jit(solution)/shard_map/ppermute | solution.py:370
  105.3 2.5 %collective-permute-start.3 = (bf16[8,32,128]{2,1,0:T(8,128)(2,1)S(1)}, bf16[8,32,128]{2,1,0:T(8,128)(2,1)S(1)}, u32[]{:S(2)}, u32[]{:S(2)}) collective-permute-start(bf16[8,32,128]{2,1,0:T(8,128)(2,1)S(1)} %all_to_all.40.parts_ref), channel_id=1, source_target_pairs={{0,1},{1,0},{2,3},{3,2},{4,5},{5,4},{6,7},{7,6},{8,9},{9,8},{10,11... | collective-permute-start | bytes 196616 | tf_op jit(solution)/shard_map/ppermute | solution.py:332
  107.8 15.7 %copy-start = (bf16[4,10,256]{2,0,1:T(4,128)(2,1)S(1)}, bf16[4,10,256]{2,0,1:T(4,128)(2,1)}, u32[]{:S(2)}) copy-start(bf16[4,10,256]{2,0,1:T(4,128)(2,1)} %param.6) | copy-start | bytes 61444
where the time goes:
time: 125 us; the launch traced here: 124 us
  blocking collectives  96.1 us (77%)
  Pallas kernels  18.6 us (15%)
  starting transfers between devices  8.51 us (7%)
    all_to_all x7, blocking collectives, exchange(): return lax.all_to_all(array, axis, 0, 0, tiled=True, **kw)  96.1 us
    ppermute x1, starting transfers between devices, body(): lax.ppermute(row_parts, 'dp', [(j, (j + half) % parts) for j in range(par...  4.3 us
    ppermute x3, starting transfers between devices, swap(): return lax.ppermute(array, 'proto', [(j, j ^ 1) for j in range(groups)])  4.22 us
    pallas_call x1, Pallas kernels, body(): call(functools.partial(student_other_kernel, stud), 'students_other_core'...  3.07 us
    pallas_call x1, Pallas kernels, body(): call(functools.partial(student_own_kernel, stud), 'students_own_core', [s...  3.06 us
    pallas_call x2, Pallas kernels, body(): call(row_kernel, 'sum_over_rows', shape((parts, protos // LANES, LANES),...  2.65 us
  transfers between devices with their start and end apart: 4, of which 1 were waited for; matrix products, arithmetic and copies ran while one was open for 0% of the time, Pallas kernels for 9%

commit v1 on v0

--- a/solution.py
+++ b/solution.py
@@ -184,7 +184,7 @@
 
 
 def pair_kernel(mine_ref, got_ref, out_ref):
-    total = mine_ref[...] + got_ref[...]
+    total = (mine_ref[...] + got_ref[...]).astype(bf16)
     for j in range(out_ref.shape[0]):
         out_ref[j] = total
 
@@ -393,20 +393,8 @@
         ],
         **work,
     )(own_rows, other_protos, acc, tot)
-    own_glob = chips * glob
-    other_exps = call(
-        functools.partial(other_core_kernel, stud, glob),
-        "teacher_other_core",
-        pltpu.VMEM((own_glob, protos), bf16),
-        flops=2 * own_glob * protos * width,
-        nbytes=2 * protos * width,
-        exps=own_glob * protos,
-    )(own_rows, other_protos)
-    got_sums, attract, total, other_exps = lax.optimization_barrier(
-        (got_sums, attract, total, other_exps)
-    )
-    other_exps = in_vmem(other_exps)
-    row_parts = call(pair_kernel, "add_halves", shape((half, protos // LANES, LANES), f32))(row_parts, got_sums)
+    got_sums, attract, total = lax.optimization_barrier((got_sums, attract, total))
+    row_parts = call(pair_kernel, "add_halves", shape((half, protos // LANES, LANES), bf16))(row_parts, got_sums)
     halves = [list(range(half)), list(range(half, parts))]
     row_parts = exchange(row_parts, "dp", axis_index_groups=halves)
 
@@ -429,7 +417,18 @@
         )(col_parts, exps)
         row_parts = exchange(row_parts, "dp")
 
+    row_parts, own_rows = lax.optimization_barrier((row_parts, own_rows))
     other_parts = swap(row_parts)
+    own_glob = chips * glob
+    other_exps = call(
+        functools.partial(other_core_kernel, stud, glob),
+        "teacher_other_core",
+        pltpu.VMEM((own_glob, protos), bf16),
+        flops=2 * own_glob * protos * width,
+        nbytes=2 * protos * width,
+        exps=own_glob * protos,
+    )(own_rows, other_protos)
+    other_exps = in_vmem(other_exps)
     work = dict(flops=2 * own_glob * protos * width, nbytes=4 * protos * width)
     repel, mass = call(
         repel_own_kernel,

time: 125 us -> 125 us (level)
  transfers between devices with their start and end apart: 4 -> 4, of which waited for: 1 -> 0; matrix products, arithmetic and copies ran while one was open for 0% -> 0% of each run, Pallas kernels for 9% -> 9%
where the time goes in v1:
time: 125 us; the launch traced here: 124 us
  blocking collectives  96.4 us (77%)
  Pallas kernels  18.6 us (15%)
  starting transfers between devices  8.51 us (7%)
    all_to_all x7, blocking collectives, exchange(): return lax.all_to_all(array, axis, 0, 0, tiled=True, **kw)  96.4 us
    ppermute x1, starting transfers between devices, body(): lax.ppermute(row_parts, 'dp', [(j, (j + half) % parts) for j in range(par...  4.3 us
    ppermute x3, starting transfers between devices, swap(): return lax.ppermute(array, 'proto', [(j, j ^ 1) for j in range(groups)])  4.22 us
    pallas_call x1, Pallas kernels, body(): call(functools.partial(student_other_kernel, stud), 'students_other_core'...  3.07 us
    pallas_call x1, Pallas kernels, body(): call(functools.partial(student_own_kernel, stud), 'students_own_core', [s...  3.06 us
    pallas_call x2, Pallas kernels, body(): call(row_kernel, 'sum_over_rows', shape((parts, protos // LANES, LANES),...  2.64 us
  transfers between devices with their start and end apart: 4, of which 0 were waited for; matrix products, arithmetic and copies ran while one was open for 0% of the time, Pallas kernels for 9%

profile of v1, /device:TPU:1, one launch (start us, length us, event | category | flops | bytes accessed | tf_op | source)
XLA Modules:
  0.0 124.3 jit_solution(15002791657923360522)
XLA Ops:
  0.6 0.9 pack_rows.1
  1.5 22.1 %all_to_all.35.own_ref = bf16[16,120,128]{2,1,0:T(8,128)(2,1)S(1)} all-to-all(bf16[16,120,128]{2,1,0:T(8,128)(2,1)S(1)} %pack_rows.1), channel_id=1, replica_groups={{0,2,4,6,8,10,12,14,16,18,20,22,24,26,28,30},{1,3,5,7,9,11,13,15,17,19,..., dimensions={0} | all-to-all | bytes 983040 | tf_op jit(solution)/shard_map/all_to_all | solution.py:314
  23.6 2.5 %collective-permute-start = (bf16[16,120,128]{2,1,0:T(8,128)(2,1)S(1)}, bf16[16,120,128]{2,1,0:T(8,128)(2,1)S(1)}, u32[]{:S(2)}, u32[]{:S(2)}) collective-permute-start(bf16[16,120,128]{2,1,0:T(8,128)(2,1)S(1)} %all_to_all.35.own_ref), channel_id=1, source_target_pairs={{0,1},{1,0},{2,3},{3,2},{4,5},{5,4},{6,7},{7,6},{8,9},{9,8},{10,11... | collective-permute-start | bytes 1474568 | tf_op jit(solution)/shard_map/ppermute | solution.py:332
  26.1 2.3 %unit_prototypes.1.unit_ref = bf16[4096,256]{1,0:T(8,128)(2,1)S(1)} custom-call(bf16[4096,256]{1,0:T(8,128)(2,1)} %protos_ref), custom_call_target="tpu_custom_call" | custom-call | flops 3145728 | bytes 4194304 | tf_op jit(solution)/shard_map/unit_prototypes/pallas_call | solution.py:345
  28.4 0.0 collective-permute-done.other_ref
  28.4 0.1 collective-permute-start.2
  28.5 1.6 %teacher_exponentials.1 = (bf16[640,4096]{1,0:T(8,128)(2,1)S(1)}, f32[32,128]{1,0:T(8,128)S(1)}) custom-call(s32[1]{0:T(128)} %bitcast.core_ref, bf16[16,120,128]{2,1,0:T(8,128)(2,1)S(1)} %all_to_all.35.own_ref, bf16[16,120,128]{2,1,0:T(8,128)(2,1)S(1)} %collective-permute-done.other_ref, bf16[4096,256]{1,0:T(8,128)(2,1)S(1)} %unit_prototypes.1.unit_ref), custom_call_target="tpu_custom_call" | custom-call | flops 1342177280 | bytes 5242880 | tf_op jit(solution)/shard_map/teacher_exponentials/pallas_call | solution.py:357
  30.1 4.3 %collective-permute-start.1 = (f32[32,128]{1,0:T(8,128)S(1)}, f32[32,128]{1,0:T(8,128)S(1)}, u32[]{:S(2)}, u32[]{:S(2)}) collective-permute-start(f32[32,128]{1,0:T(8,128)S(1)} %get-tuple-element.32.mine_ref), channel_id=1, source_target_pairs={{0,128},{32,160},{64,192},{96,224},{128,0},{160,32},{192,64},{224,... | collective-permute-start | bytes 49160 | tf_op jit(solution)/shard_map/ppermute | solution.py:370
  34.4 3.1 %students_own_core.1 = (f32[640,256]{1,0:T(8,128)S(1)}, f32[640,128]{1,0:T(8,128)S(1)}) custom-call(bf16[16,120,128]{2,1,0:T(8,128)(2,1)S(1)} %all_to_all.35.own_ref, bf16[4096,256]{1,0:T(8,128)(2,1)S(1)} %unit_prototypes.1.unit_ref), custom_call_target="tpu_custom_call" | custom-call | flops 2684354560 | bytes 2097152 | tf_op jit(solution)/shard_map/students_own_core/pallas_call | solution.py:378
  37.5 0.0 collective-permute-done.2.unit_ref
  37.5 3.1 %students_other_core.1 = (bf16[16,80,128]{2,1,0:T(8,128)(2,1)S(1)}, f32[16,1,128]{2,1,0:T(1,128)S(1)}) custom-call(bf16[16,120,128]{2,1,0:T(8,128)(2,1)S(1)} %all_to_all.35.own_ref, bf16[4096,256]{1,0:T(8,128)(2,1)S(1)} %collective-permute-done.2.unit_ref, f32[640,256]{1,0:T(8,128)S(1)} %get-tuple-element.34.start_acc, ...), custom_call_target="tpu_custom_call" | custom-call | flops 2684354560 | bytes 2097152 | tf_op jit(solution)/shard_map/students_other_core/pallas_call | solution.py:385
  40.6 0.0 collective-permute-done.1.got_ref
  40.6 8.3 %all_to_all.36.parts_ref = bf16[4,32,128]{2,1,0:T(8,128)(2,1)S(1)} all-to-all(bf16[4,32,128]{2,1,0:T(8,128)(2,1)S(1)} %add_halves.1), channel_id=1, replica_groups={{0,32,64,96},{128,160,192,224},{1,33,65,97},{129,161,193,225},{2,34,66,..., dimensions={0} | all-to-all | bytes 65536 | tf_op jit(solution)/shard_map/all_to_all | solution.py:314
  48.9 1.1 sum_over_prototypes.2
  50.0 14.3 %all_to_all.37.parts_ref = f32[32,1,640]{2,1,0:T(1,128)S(1)} all-to-all(f32[32,1,640]{2,1,0:T(1,128)S(1)} %sum_over_prototypes.2), channel_id=1, replica_groups=mesh['dp'=8,'proto'=32] {'proto'}, dimensions={0} | all-to-all | bytes 163840 | tf_op jit(solution)/shard_map/all_to_all | solution.py:314
  64.4 1.3 %sum_over_rows.2 = bf16[8,32,128]{2,1,0:T(8,128)(2,1)S(1)} custom-call(f32[32,1,640]{2,1,0:T(1,128)S(1)} %all_to_all.37.parts_ref, bf16[640,4096]{1,0:T(8,128)(2,1)S(1)} %get-tuple-element.39.exp_ref), custom_call_target="tpu_custom_call" | custom-call | flops 5242880 | bytes 5242880 | tf_op jit(solution)/shard_map/sum_over_rows/pallas_call | solution.py:410
  65.7 12.0 %all_to_all.38.parts_ref = bf16[8,32,128]{2,1,0:T(8,128)(2,1)S(1)} all-to-all(bf16[8,32,128]{2,1,0:T(8,128)(2,1)S(1)} %sum_over_rows.2), channel_id=1, replica_groups=mesh['dp'=8,'proto'=32] {'dp'}, dimensions={0} | all-to-all | bytes 131072 | tf_op jit(solution)/shard_map/all_to_all | solution.py:314
  77.6 1.1 sum_over_prototypes.3
  78.8 12.7 %all_to_all.39.parts_ref = f32[32,1,640]{2,1,0:T(1,128)S(1)} all-to-all(f32[32,1,640]{2,1,0:T(1,128)S(1)} %sum_over_prototypes.3), channel_id=1, replica_groups=mesh['dp'=8,'proto'=32] {'proto'}, dimensions={0} | all-to-all | bytes 163840 | tf_op jit(solution)/shard_map/all_to_all | solution.py:314
  91.5 1.3 %sum_over_rows.3 = bf16[8,32,128]{2,1,0:T(8,128)(2,1)S(1)} custom-call(f32[32,1,640]{2,1,0:T(1,128)S(1)} %all_to_all.39.parts_ref, bf16[640,4096]{1,0:T(8,128)(2,1)S(1)} %get-tuple-element.39.exp_ref), custom_call_target="tpu_custom_call" | custom-call | flops 5242880 | bytes 5242880 | tf_op jit(solution)/shard_map/sum_over_rows/pallas_call | solution.py:410
  92.8 11.5 %all_to_all.40.parts_ref = bf16[8,32,128]{2,1,0:T(8,128)(2,1)S(1)} all-to-all(bf16[8,32,128]{2,1,0:T(8,128)(2,1)S(1)} %sum_over_rows.3), channel_id=1, replica_groups=mesh['dp'=8,'proto'=32] {'dp'}, dimensions={0} | all-to-all | bytes 131072 | tf_op jit(solution)/shard_map/all_to_all | solution.py:314
  104.3 1.6 %collective-permute-start.3 = (bf16[8,32,128]{2,1,0:T(8,128)(2,1)S(1)}, bf16[8,32,128]{2,1,0:T(8,128)(2,1)S(1)}, u32[]{:S(2)}, u32[]{:S(2)}) collective-permute-start(bf16[8,32,128]{2,1,0:T(8,128)(2,1)S(1)} %all_to_all.40.parts_ref), channel_id=1, source_target_pairs={{0,1},{1,0},{2,3},{3,2},{4,5},{5,4},{6,7},{7,6},{8,9},{9,8},{10,11... | collective-permute-start | bytes 196616 | tf_op jit(solution)/shard_map/ppermute | solution.py:332
  105.9 0.6 repel_own_core.1
  106.5 0.8 teacher_other_core.1.exp_ref
  107.3 0.0 collective-permute-done.3.parts_ref
  107.3 0.0 copy-start
  107.3 0.6 repel_other_core.1
  107.9 15.6 %all_to_all.41.back_ref = bf16[16,104,128]{2,1,0:T(8,128)(2,1)S(1)} all-to-all(bf16[16,104,128]{2,1,0:T(8,128)(2,1)S(1)} %repel_other_core.1), channel_id=1, replica_groups={{0,2,4,6,8,10,12,14,16,18,20,22,24,26,28,30},{1,3,5,7,9,11,13,15,17,19,..., dimensions={0} | all-to-all | bytes 851968 | tf_op jit(solution)/shard_map/all_to_all | solution.py:314
  123.4 0.0 copy-done
  123.4 0.8 gradients.1
  (1 shorter events, 0.0 us)
Async XLA Ops:
  23.6 4.8 %collective-permute-start = (bf16[16,120,128]{2,1,0:T(8,128)(2,1)S(1)}, bf16[16,120,128]{2,1,0:T(8,128)(2,1)S(1)}, u32[]{:S(2)}, u32[]{:S(2)}) collective-permute-start(bf16[16,120,128]{2,1,0:T(8,128)(2,1)S(1)} %all_to_all.35.own_ref), channel_id=1, source_target_pairs={{0,1},{1,0},{2,3},{3,2},{4,5},{5,4},{6,7},{7,6},{8,9},{9,8},{10,11... | collective-permute-start | bytes 1474568 | tf_op jit(solution)/shard_map/ppermute | solution.py:332
  28.4 9.1 %collective-permute-start.2 = (bf16[4096,256]{1,0:T(8,128)(2,1)S(1)}, bf16[4096,256]{1,0:T(8,128)(2,1)S(1)}, u32[]{:S(2)}, u32[]{:S(2)}) collective-permute-start(bf16[4096,256]{1,0:T(8,128)(2,1)S(1)} %unit_prototypes.1.unit_ref), channel_id=1, source_target_pairs={{0,1},{1,0},{2,3},{3,2},{4,5},{5,4},{6,7},{7,6},{8,9},{9,8},{10,11... | collective-permute-start | bytes 6291464 | tf_op jit(solution)/shard_map/ppermute | solution.py:332
  30.1 10.5 %collective-permute-start.1 = (f32[32,128]{1,0:T(8,128)S(1)}, f32[32,128]{1,0:T(8,128)S(1)}, u32[]{:S(2)}, u32[]{:S(2)}) collective-permute-start(f32[32,128]{1,0:T(8,128)S(1)} %get-tuple-element.32.mine_ref), channel_id=1, source_target_pairs={{0,128},{32,160},{64,192},{96,224},{128,0},{160,32},{192,64},{224,... | collective-permute-start | bytes 49160 | tf_op jit(solution)/shard_map/ppermute | solution.py:370
  104.3 3.0 %collective-permute-start.3 = (bf16[8,32,128]{2,1,0:T(8,128)(2,1)S(1)}, bf16[8,32,128]{2,1,0:T(8,128)(2,1)S(1)}, u32[]{:S(2)}, u32[]{:S(2)}) collective-permute-start(bf16[8,32,128]{2,1,0:T(8,128)(2,1)S(1)} %all_to_all.40.parts_ref), channel_id=1, source_target_pairs={{0,1},{1,0},{2,3},{3,2},{4,5},{5,4},{6,7},{7,6},{8,9},{9,8},{10,11... | collective-permute-start | bytes 196616 | tf_op jit(solution)/shard_map/ppermute | solution.py:332
  107.3 16.1 %copy-start = (bf16[4,10,256]{2,0,1:T(4,128)(2,1)S(1)}, bf16[4,10,256]{2,0,1:T(4,128)(2,1)}, u32[]{:S(2)}) copy-start(bf16[4,10,256]{2,0,1:T(4,128)(2,1)} %param.6) | copy-start | bytes 61444

commit v2 on v1

--- a/solution.py
+++ b/solution.py
@@ -102,7 +102,7 @@
     return jnp.where(is_first, own, other), jnp.where(is_first, other, own)
 
 
-def teacher_kernel(stud, glob, core_ref, own_ref, other_ref, unit_ref, exp_ref, sums_ref):
+def teacher_kernel(stud, glob, core_ref, own_ref, other_ref, unit_ref, exp_ref, sums_ref, line_ref):
     chips, _, half = own_ref.shape
     width = 2 * half
     at = 2 * stud
@@ -126,7 +126,10 @@
         sums = jnp.sum(exps, axis=0, keepdims=True)
         for k in range(step // LANES):
             at = start // LANES + k
-            sums_ref[at : at + 1, :] = sums[:, k * LANES : (k + 1) * LANES]
+            line_ref[at : at + 1, :] = sums[:, k * LANES : (k + 1) * LANES]
+    sums = line_ref[...].astype(bf16)
+    for j in range(sums_ref.shape[0]):
+        sums_ref[j] = sums
 
 
 def other_core_kernel(stud, glob, own_ref, unit_ref, exp_ref):
@@ -183,22 +186,16 @@
     )
 
 
-def pair_kernel(mine_ref, got_ref, out_ref):
-    total = (mine_ref[...] + got_ref[...]).astype(bf16)
-    for j in range(out_ref.shape[0]):
-        out_ref[j] = total
-
-
-def proto_scale_of(parts_ref):
-    total = parts_ref[0].astype(f32)
-    for j in range(1, parts_ref.shape[0]):
-        total = total + parts_ref[j].astype(f32)
+def proto_scale_of(*parts_refs):
+    parts = [ref[j].astype(f32) for ref in parts_refs for j in range(ref.shape[0])]
+    total = sum(parts[1:], parts[0])
     scale = 1.0 / total
     return jnp.concatenate([scale[k : k + 1, :] for k in range(scale.shape[0])], axis=1)
 
 
-def col_kernel(parts_ref, exp_ref, out_ref):
-    scale = proto_scale_of(parts_ref)
+def col_kernel(*refs):
+    *parts_refs, exp_ref, out_ref = refs
+    scale = proto_scale_of(*parts_refs)
     rows, cols = exp_ref.shape
     lines = []
     for g in range(rows // LANES):
@@ -354,19 +351,22 @@
 
     other_rows, unit_protos = lax.optimization_barrier((other_rows, unit_protos))
     other_protos = swap(unit_protos)
+    half = parts // 2
     exps, row_parts = call(
         functools.partial(teacher_kernel, stud, glob),
         "teacher_exponentials",
-        [pltpu.VMEM((teach_rows, protos), bf16), shape((protos // LANES, LANES), f32)],
+        [pltpu.VMEM((teach_rows, protos), bf16), shape((half, protos // LANES, LANES), bf16)],
         in_specs=[scalar, vmem, vmem, vmem],
+        scratch_shapes=[pltpu.VMEM((protos // LANES, LANES), f32)],
         flops=2 * teach_rows * protos * width,
         nbytes=2 * teach_rows * protos,
         exps=teach_rows * protos,
     )(core, own_rows, other_rows, unit_protos)
     exps = in_vmem(exps)
 
+    halves = [list(range(half)), list(range(half, parts))]
+    row_parts = exchange(row_parts, "dp", axis_index_groups=halves)
     row_parts, own_rows = lax.optimization_barrier((row_parts, own_rows))
-    half = parts // 2
     got_sums = lax.ppermute(row_parts, "dp", [(j, (j + half) % parts) for j in range(parts)])
     own_students = chips * stud
     work = dict(
@@ -394,9 +394,7 @@
         **work,
     )(own_rows, other_protos, acc, tot)
     got_sums, attract, total = lax.optimization_barrier((got_sums, attract, total))
-    row_parts = call(pair_kernel, "add_halves", shape((half, protos // LANES, LANES), bf16))(row_parts, got_sums)
-    halves = [list(range(half)), list(range(half, parts))]
-    row_parts = exchange(row_parts, "dp", axis_index_groups=halves)
+    row_parts = (row_parts, got_sums)
 
     for iteration in range(SINK_ITERS - 1):
         col_parts = call(
@@ -405,7 +403,7 @@
             shape((groups, 1, teach_rows), f32),
             flops=2 * teach_rows * protos,
             nbytes=2 * teach_rows * protos,
-        )(row_parts, exps)
+        )(*row_parts, exps)
         col_parts = exchange(col_parts, "proto")
         row_parts = call(
             row_kernel,
@@ -415,8 +413,9 @@
             flops=2 * teach_rows * protos,
             nbytes=2 * teach_rows * protos,
         )(col_parts, exps)
-        row_parts = exchange(row_parts, "dp")
-
+        row_parts = (exchange(row_parts, "dp"),)
+
+    (row_parts,) = row_parts
     row_parts, own_rows = lax.optimization_barrier((row_parts, own_rows))
     other_parts = swap(row_parts)
     own_glob = chips * glob

time: 125 us -> 125 us (level)
  no operation moved by 1% of the time
where the time goes in v2:
time: 125 us; the launch traced here: 124 us
  blocking collectives  96.6 us (77%)
  Pallas kernels  18.6 us (15%)
  starting transfers between devices  8.44 us (7%)
    all_to_all x7, blocking collectives, exchange(): return lax.all_to_all(array, axis, 0, 0, tiled=True, **kw)  96.6 us
    ppermute x1, starting transfers between devices, body(): lax.ppermute(row_parts, 'dp', [(j, (j + half) % parts) for j in range(par...  4.22 us
    ppermute x3, starting transfers between devices, swap(): return lax.ppermute(array, 'proto', [(j, j ^ 1) for j in range(groups)])  4.22 us
    pallas_call x1, Pallas kernels, body(): call(functools.partial(student_other_kernel, stud), 'students_other_core'...  3.07 us
    pallas_call x1, Pallas kernels, body(): call(functools.partial(student_own_kernel, stud), 'students_own_core', [s...  3.06 us
    pallas_call x2, Pallas kernels, body(): call(row_kernel, 'sum_over_rows', shape((parts, protos // LANES, LANES),...  2.64 us
  transfers between devices with their start and end apart: 4, of which 0 were waited for; matrix products, arithmetic and copies ran while one was open for 0% of the time, Pallas kernels for 9%

profile of v2, /device:TPU:1, one launch (start us, length us, event | category | flops | bytes accessed | tf_op | source)
XLA Modules:
  0.0 124.5 jit_solution(11119197987526611602)
XLA Ops:
  0.6 0.9 pack_rows.1
  1.5 22.1 %all_to_all.35.own_ref = bf16[16,120,128]{2,1,0:T(8,128)(2,1)S(1)} all-to-all(bf16[16,120,128]{2,1,0:T(8,128)(2,1)S(1)} %pack_rows.1), channel_id=1, replica_groups={{0,2,4,6,8,10,12,14,16,18,20,22,24,26,28,30},{1,3,5,7,9,11,13,15,17,19,..., dimensions={0} | all-to-all | bytes 983040 | tf_op jit(solution)/shard_map/all_to_all | solution.py:311
  23.6 2.5 %collective-permute-start = (bf16[16,120,128]{2,1,0:T(8,128)(2,1)S(1)}, bf16[16,120,128]{2,1,0:T(8,128)(2,1)S(1)}, u32[]{:S(2)}, u32[]{:S(2)}) collective-permute-start(bf16[16,120,128]{2,1,0:T(8,128)(2,1)S(1)} %all_to_all.35.own_ref), channel_id=1, source_target_pairs={{0,1},{1,0},{2,3},{3,2},{4,5},{5,4},{6,7},{7,6},{8,9},{9,8},{10,11... | collective-permute-start | bytes 1474568 | tf_op jit(solution)/shard_map/ppermute | solution.py:329
  26.1 2.3 %unit_prototypes.1.unit_ref = bf16[4096,256]{1,0:T(8,128)(2,1)S(1)} custom-call(bf16[4096,256]{1,0:T(8,128)(2,1)} %protos_ref), custom_call_target="tpu_custom_call" | custom-call | flops 3145728 | bytes 4194304 | tf_op jit(solution)/shard_map/unit_prototypes/pallas_call | solution.py:342
  28.4 0.0 collective-permute-done.other_ref
  28.4 0.1 collective-permute-start.2
  28.5 1.6 %teacher_exponentials.1 = (bf16[640,4096]{1,0:T(8,128)(2,1)S(1)}, bf16[4,32,128]{2,1,0:T(8,128)(2,1)S(1)}) custom-call(s32[1]{0:T(128)} %bitcast.core_ref, bf16[16,120,128]{2,1,0:T(8,128)(2,1)S(1)} %all_to_all.35.own_ref, bf16[16,120,128]{2,1,0:T(8,128)(2,1)S(1)} %collective-permute-done.other_ref, bf16[4096,256]{1,0:T(8,128)(2,1)S(1)} %unit_prototypes.1.unit_ref), custom_call_target="tpu_custom_call" | custom-call | flops 1342177280 | bytes 5242880 | tf_op jit(solution)/shard_map/teacher_exponentials/pallas_call | solution.py:355
  30.1 8.3 %all_to_all.36.refs_0_ = bf16[4,32,128]{2,1,0:T(8,128)(2,1)S(1)} all-to-all(bf16[4,32,128]{2,1,0:T(8,128)(2,1)S(1)} %get-tuple-element.31), channel_id=1, replica_groups={{0,32,64,96},{128,160,192,224},{1,33,65,97},{129,161,193,225},{2,34,66,..., dimensions={0} | all-to-all | bytes 65536 | tf_op jit(solution)/shard_map/all_to_all | solution.py:311
  38.4 4.2 %collective-permute-start.1 = (bf16[4,32,128]{2,1,0:T(8,128)(2,1)S(1)}, bf16[4,32,128]{2,1,0:T(8,128)(2,1)S(1)}, u32[]{:S(2)}, u32[]{:S(2)}) collective-permute-start(bf16[4,32,128]{2,1,0:T(8,128)(2,1)S(1)} %all_to_all.36.refs_0_), channel_id=1, source_target_pairs={{0,128},{32,160},{64,192},{96,224},{128,0},{160,32},{192,64},{224,... | collective-permute-start | bytes 98312 | tf_op jit(solution)/shard_map/ppermute | solution.py:370
  42.6 3.1 %students_own_core.1 = (f32[640,256]{1,0:T(8,128)S(1)}, f32[640,128]{1,0:T(8,128)S(1)}) custom-call(bf16[16,120,128]{2,1,0:T(8,128)(2,1)S(1)} %all_to_all.35.own_ref, bf16[4096,256]{1,0:T(8,128)(2,1)S(1)} %unit_prototypes.1.unit_ref), custom_call_target="tpu_custom_call" | custom-call | flops 2684354560 | bytes 2097152 | tf_op jit(solution)/shard_map/students_own_core/pallas_call | solution.py:378
  45.7 0.0 collective-permute-done.2.unit_ref
  45.7 3.1 %students_other_core.1 = (bf16[16,80,128]{2,1,0:T(8,128)(2,1)S(1)}, f32[16,1,128]{2,1,0:T(1,128)S(1)}) custom-call(bf16[16,120,128]{2,1,0:T(8,128)(2,1)S(1)} %all_to_all.35.own_ref, bf16[4096,256]{1,0:T(8,128)(2,1)S(1)} %collective-permute-done.2.unit_ref, f32[640,256]{1,0:T(8,128)S(1)} %get-tuple-element.34.start_acc, ...), custom_call_target="tpu_custom_call" | custom-call | flops 2684354560 | bytes 2097152 | tf_op jit(solution)/shard_map/students_other_core/pallas_call | solution.py:385
  48.8 0.0 collective-permute-done.1.refs_1_
  48.8 1.2 sum_over_prototypes.2
  50.0 14.3 %all_to_all.37.parts_ref = f32[32,1,640]{2,1,0:T(1,128)S(1)} all-to-all(f32[32,1,640]{2,1,0:T(1,128)S(1)} %sum_over_prototypes.2), channel_id=1, replica_groups=mesh['dp'=8,'proto'=32] {'proto'}, dimensions={0} | all-to-all | bytes 163840 | tf_op jit(solution)/shard_map/all_to_all | solution.py:311
  64.3 1.3 %sum_over_rows.2 = bf16[8,32,128]{2,1,0:T(8,128)(2,1)S(1)} custom-call(f32[32,1,640]{2,1,0:T(1,128)S(1)} %all_to_all.37.parts_ref, bf16[640,4096]{1,0:T(8,128)(2,1)S(1)} %get-tuple-element.39.refs_2_.exp_ref.refs_1_), custom_call_target="tpu_custom_call" | custom-call | flops 5242880 | bytes 5242880 | tf_op jit(solution)/shard_map/sum_over_rows/pallas_call | solution.py:408
  65.6 12.2 %all_to_all.38.refs_0_ = bf16[8,32,128]{2,1,0:T(8,128)(2,1)S(1)} all-to-all(bf16[8,32,128]{2,1,0:T(8,128)(2,1)S(1)} %sum_over_rows.2), channel_id=1, replica_groups=mesh['dp'=8,'proto'=32] {'dp'}, dimensions={0} | all-to-all | bytes 131072 | tf_op jit(solution)/shard_map/all_to_all | solution.py:311
  77.8 1.2 sum_over_prototypes.3
  78.9 12.7 %all_to_all.39.parts_ref = f32[32,1,640]{2,1,0:T(1,128)S(1)} all-to-all(f32[32,1,640]{2,1,0:T(1,128)S(1)} %sum_over_prototypes.3), channel_id=1, replica_groups=mesh['dp'=8,'proto'=32] {'proto'}, dimensions={0} | all-to-all | bytes 163840 | tf_op jit(solution)/shard_map/all_to_all | solution.py:311
  91.7 1.3 %sum_over_rows.3 = bf16[8,32,128]{2,1,0:T(8,128)(2,1)S(1)} custom-call(f32[32,1,640]{2,1,0:T(1,128)S(1)} %all_to_all.39.parts_ref, bf16[640,4096]{1,0:T(8,128)(2,1)S(1)} %get-tuple-element.39.refs_2_.exp_ref.refs_1_), custom_call_target="tpu_custom_call" | custom-call | flops 5242880 | bytes 5242880 | tf_op jit(solution)/shard_map/sum_over_rows/pallas_call | solution.py:408
  93.0 11.5 %all_to_all.40.parts_ref = bf16[8,32,128]{2,1,0:T(8,128)(2,1)S(1)} all-to-all(bf16[8,32,128]{2,1,0:T(8,128)(2,1)S(1)} %sum_over_rows.3), channel_id=1, replica_groups=mesh['dp'=8,'proto'=32] {'dp'}, dimensions={0} | all-to-all | bytes 131072 | tf_op jit(solution)/shard_map/all_to_all | solution.py:311
  104.5 1.6 %collective-permute-start.3 = (bf16[8,32,128]{2,1,0:T(8,128)(2,1)S(1)}, bf16[8,32,128]{2,1,0:T(8,128)(2,1)S(1)}, u32[]{:S(2)}, u32[]{:S(2)}) collective-permute-start(bf16[8,32,128]{2,1,0:T(8,128)(2,1)S(1)} %all_to_all.40.parts_ref), channel_id=1, source_target_pairs={{0,1},{1,0},{2,3},{3,2},{4,5},{5,4},{6,7},{7,6},{8,9},{9,8},{10,11... | collective-permute-start | bytes 196616 | tf_op jit(solution)/shard_map/ppermute | solution.py:329
  106.0 0.6 repel_own_core.1
  106.6 0.8 teacher_other_core.1.exp_ref
  107.5 0.0 collective-permute-done.3.parts_ref
  107.5 0.0 copy-start
  107.5 0.6 repel_other_core.1
  108.0 15.6 %all_to_all.41.back_ref = bf16[16,104,128]{2,1,0:T(8,128)(2,1)S(1)} all-to-all(bf16[16,104,128]{2,1,0:T(8,128)(2,1)S(1)} %repel_other_core.1), channel_id=1, replica_groups={{0,2,4,6,8,10,12,14,16,18,20,22,24,26,28,30},{1,3,5,7,9,11,13,15,17,19,..., dimensions={0} | all-to-all | bytes 851968 | tf_op jit(solution)/shard_map/all_to_all | solution.py:311
  123.6 0.0 copy-done
  123.6 0.8 gradients.1
Async XLA Ops:
  23.6 4.8 %collective-permute-start = (bf16[16,120,128]{2,1,0:T(8,128)(2,1)S(1)}, bf16[16,120,128]{2,1,0:T(8,128)(2,1)S(1)}, u32[]{:S(2)}, u32[]{:S(2)}) collective-permute-start(bf16[16,120,128]{2,1,0:T(8,128)(2,1)S(1)} %all_to_all.35.own_ref), channel_id=1, source_target_pairs={{0,1},{1,0},{2,3},{3,2},{4,5},{5,4},{6,7},{7,6},{8,9},{9,8},{10,11... | collective-permute-start | bytes 1474568 | tf_op jit(solution)/shard_map/ppermute | solution.py:329
  28.4 17.3 %collective-permute-start.2 = (bf16[4096,256]{1,0:T(8,128)(2,1)S(1)}, bf16[4096,256]{1,0:T(8,128)(2,1)S(1)}, u32[]{:S(2)}, u32[]{:S(2)}) collective-permute-start(bf16[4096,256]{1,0:T(8,128)(2,1)S(1)} %unit_prototypes.1.unit_ref), channel_id=1, source_target_pairs={{0,1},{1,0},{2,3},{3,2},{4,5},{5,4},{6,7},{7,6},{8,9},{9,8},{10,11... | collective-permute-start | bytes 6291464 | tf_op jit(solution)/shard_map/ppermute | solution.py:329
  38.4 10.4 %collective-permute-start.1 = (bf16[4,32,128]{2,1,0:T(8,128)(2,1)S(1)}, bf16[4,32,128]{2,1,0:T(8,128)(2,1)S(1)}, u32[]{:S(2)}, u32[]{:S(2)}) collective-permute-start(bf16[4,32,128]{2,1,0:T(8,128)(2,1)S(1)} %all_to_all.36.refs_0_), channel_id=1, source_target_pairs={{0,128},{32,160},{64,192},{96,224},{128,0},{160,32},{192,64},{224,... | collective-permute-start | bytes 98312 | tf_op jit(solution)/shard_map/ppermute | solution.py:370
  104.5 3.0 %collective-permute-start.3 = (bf16[8,32,128]{2,1,0:T(8,128)(2,1)S(1)}, bf16[8,32,128]{2,1,0:T(8,128)(2,1)S(1)}, u32[]{:S(2)}, u32[]{:S(2)}) collective-permute-start(bf16[8,32,128]{2,1,0:T(8,128)(2,1)S(1)} %all_to_all.40.parts_ref), channel_id=1, source_target_pairs={{0,1},{1,0},{2,3},{3,2},{4,5},{5,4},{6,7},{7,6},{8,9},{9,8},{10,11... | collective-permute-start | bytes 196616 | tf_op jit(solution)/shard_map/ppermute | solution.py:329
  107.5 16.2 %copy-start = (bf16[4,10,256]{2,0,1:T(4,128)(2,1)S(1)}, bf16[4,10,256]{2,0,1:T(4,128)(2,1)}, u32[]{:S(2)}) copy-start(bf16[4,10,256]{2,0,1:T(4,128)(2,1)} %param.6) | copy-start | bytes 61444

commit v3 on v1

--- a/solution.py
+++ b/solution.py
@@ -90,9 +90,12 @@
     for j in range(parts):
         here = pl.ds(j * rows, rows)
         copies.append(pltpu.make_async_copy(protos_ref.at[here], raw_ref.at[here], sems.at[j]))
-        copies[j].start()
+    for copy in copies[:3]:
+        copy.start()
     for j in range(parts):
         copies[j].wait()
+        if j + 3 < parts:
+            copies[j + 3].start()
         here = slice(j * rows, (j + 1) * rows)
         out_ref[here, :] = unit(raw_ref[here, :].astype(f32)).astype(bf16)
 

time: 125 us -> 126 us (level)
  transfers between devices with their start and end apart: 4 -> 4, of which waited for: 0 -> 0; matrix products, arithmetic and copies ran while one was open for 0% -> 0% of each run, Pallas kernels for 9% -> 10%
where the time goes in v3:
time: 126 us; the launch traced here: 125 us
  blocking collectives  96.4 us (77%)
  Pallas kernels  19.6 us (16%)
  starting transfers between devices  8.51 us (7%)
    all_to_all x7, blocking collectives, exchange(): return lax.all_to_all(array, axis, 0, 0, tiled=True, **kw)  96.4 us
    ppermute x1, starting transfers between devices, body(): lax.ppermute(row_parts, 'dp', [(j, (j + half) % parts) for j in range(par...  4.3 us
    ppermute x3, starting transfers between devices, swap(): return lax.ppermute(array, 'proto', [(j, j ^ 1) for j in range(groups)])  4.22 us
    pallas_call x1, Pallas kernels, body(): call(unit_kernel, 'unit_prototypes', shape((protos, width), bf16), in_spe...  3.3 us
    pallas_call x1, Pallas kernels, body(): call(functools.partial(student_other_kernel, stud), 'students_other_core'...  3.07 us
    pallas_call x1, Pallas kernels, body(): call(functools.partial(student_own_kernel, stud), 'students_own_core', [s...  3.06 us
    pallas_call x2, Pallas kernels, body(): call(row_kernel, 'sum_over_rows', shape((parts, protos // LANES, LANES),...  2.64 us
  transfers between devices with their start and end apart: 4, of which 0 were waited for; matrix products, arithmetic and copies ran while one was open for 0% of the time, Pallas kernels for 10%

profile of v3, /device:TPU:1, one launch (start us, length us, event | category | flops | bytes accessed | tf_op | source)
XLA Modules:
  0.0 125.3 jit_solution(16257740966877459216)
XLA Ops:
  0.6 0.9 pack_rows.1
  1.5 22.1 %all_to_all.35.own_ref = bf16[16,120,128]{2,1,0:T(8,128)(2,1)S(1)} all-to-all(bf16[16,120,128]{2,1,0:T(8,128)(2,1)S(1)} %pack_rows.1), channel_id=1, replica_groups={{0,2,4,6,8,10,12,14,16,18,20,22,24,26,28,30},{1,3,5,7,9,11,13,15,17,19,..., dimensions={0} | all-to-all | bytes 983040 | tf_op jit(solution)/shard_map/all_to_all | solution.py:317
  23.6 2.5 %collective-permute-start = (bf16[16,120,128]{2,1,0:T(8,128)(2,1)S(1)}, bf16[16,120,128]{2,1,0:T(8,128)(2,1)S(1)}, u32[]{:S(2)}, u32[]{:S(2)}) collective-permute-start(bf16[16,120,128]{2,1,0:T(8,128)(2,1)S(1)} %all_to_all.35.own_ref), channel_id=1, source_target_pairs={{0,1},{1,0},{2,3},{3,2},{4,5},{5,4},{6,7},{7,6},{8,9},{9,8},{10,11... | collective-permute-start | bytes 1474568 | tf_op jit(solution)/shard_map/ppermute | solution.py:335
  26.1 3.3 %unit_prototypes.1.unit_ref = bf16[4096,256]{1,0:T(8,128)(2,1)S(1)} custom-call(bf16[4096,256]{1,0:T(8,128)(2,1)} %protos_ref), custom_call_target="tpu_custom_call" | custom-call | flops 3145728 | bytes 4194304 | tf_op jit(solution)/shard_map/unit_prototypes/pallas_call | solution.py:348
  29.4 0.0 collective-permute-done.other_ref
  29.5 0.1 collective-permute-start.2
  29.6 1.6 %teacher_exponentials.1 = (bf16[640,4096]{1,0:T(8,128)(2,1)S(1)}, f32[32,128]{1,0:T(8,128)S(1)}) custom-call(s32[1]{0:T(128)} %bitcast.core_ref, bf16[16,120,128]{2,1,0:T(8,128)(2,1)S(1)} %all_to_all.35.own_ref, bf16[16,120,128]{2,1,0:T(8,128)(2,1)S(1)} %collective-permute-done.other_ref, bf16[4096,256]{1,0:T(8,128)(2,1)S(1)} %unit_prototypes.1.unit_ref), custom_call_target="tpu_custom_call" | custom-call | flops 1342177280 | bytes 5242880 | tf_op jit(solution)/shard_map/teacher_exponentials/pallas_call | solution.py:360
  31.2 4.3 %collective-permute-start.1 = (f32[32,128]{1,0:T(8,128)S(1)}, f32[32,128]{1,0:T(8,128)S(1)}, u32[]{:S(2)}, u32[]{:S(2)}) collective-permute-start(f32[32,128]{1,0:T(8,128)S(1)} %get-tuple-element.32.mine_ref), channel_id=1, source_target_pairs={{0,128},{32,160},{64,192},{96,224},{128,0},{160,32},{192,64},{224,... | collective-permute-start | bytes 49160 | tf_op jit(solution)/shard_map/ppermute | solution.py:373
  35.5 3.1 %students_own_core.1 = (f32[640,256]{1,0:T(8,128)S(1)}, f32[640,128]{1,0:T(8,128)S(1)}) custom-call(bf16[16,120,128]{2,1,0:T(8,128)(2,1)S(1)} %all_to_all.35.own_ref, bf16[4096,256]{1,0:T(8,128)(2,1)S(1)} %unit_prototypes.1.unit_ref), custom_call_target="tpu_custom_call" | custom-call | flops 2684354560 | bytes 2097152 | tf_op jit(solution)/shard_map/students_own_core/pallas_call | solution.py:381
  38.5 0.0 collective-permute-done.2.unit_ref
  38.6 3.1 %students_other_core.1 = (bf16[16,80,128]{2,1,0:T(8,128)(2,1)S(1)}, f32[16,1,128]{2,1,0:T(1,128)S(1)}) custom-call(bf16[16,120,128]{2,1,0:T(8,128)(2,1)S(1)} %all_to_all.35.own_ref, bf16[4096,256]{1,0:T(8,128)(2,1)S(1)} %collective-permute-done.2.unit_ref, f32[640,256]{1,0:T(8,128)S(1)} %get-tuple-element.34.start_acc, ...), custom_call_target="tpu_custom_call" | custom-call | flops 2684354560 | bytes 2097152 | tf_op jit(solution)/shard_map/students_other_core/pallas_call | solution.py:388
  41.6 0.0 collective-permute-done.1.got_ref
  41.7 8.3 %all_to_all.36.parts_ref = bf16[4,32,128]{2,1,0:T(8,128)(2,1)S(1)} all-to-all(bf16[4,32,128]{2,1,0:T(8,128)(2,1)S(1)} %add_halves.1), channel_id=1, replica_groups={{0,32,64,96},{128,160,192,224},{1,33,65,97},{129,161,193,225},{2,34,66,..., dimensions={0} | all-to-all | bytes 65536 | tf_op jit(solution)/shard_map/all_to_all | solution.py:317
  50.0 1.1 sum_over_prototypes.2
  51.1 14.3 %all_to_all.37.parts_ref = f32[32,1,640]{2,1,0:T(1,128)S(1)} all-to-all(f32[32,1,640]{2,1,0:T(1,128)S(1)} %sum_over_prototypes.2), channel_id=1, replica_groups=mesh['dp'=8,'proto'=32] {'proto'}, dimensions={0} | all-to-all | bytes 163840 | tf_op jit(solution)/shard_map/all_to_all | solution.py:317
  65.4 1.3 %sum_over_rows.2 = bf16[8,32,128]{2,1,0:T(8,128)(2,1)S(1)} custom-call(f32[32,1,640]{2,1,0:T(1,128)S(1)} %all_to_all.37.parts_ref, bf16[640,4096]{1,0:T(8,128)(2,1)S(1)} %get-tuple-element.39.exp_ref), custom_call_target="tpu_custom_call" | custom-call | flops 5242880 | bytes 5242880 | tf_op jit(solution)/shard_map/sum_over_rows/pallas_call | solution.py:413
  66.7 12.0 %all_to_all.38.parts_ref = bf16[8,32,128]{2,1,0:T(8,128)(2,1)S(1)} all-to-all(bf16[8,32,128]{2,1,0:T(8,128)(2,1)S(1)} %sum_over_rows.2), channel_id=1, replica_groups=mesh['dp'=8,'proto'=32] {'dp'}, dimensions={0} | all-to-all | bytes 131072 | tf_op jit(solution)/shard_map/all_to_all | solution.py:317
  78.7 1.1 sum_over_prototypes.3
  79.8 12.7 %all_to_all.39.parts_ref = f32[32,1,640]{2,1,0:T(1,128)S(1)} all-to-all(f32[32,1,640]{2,1,0:T(1,128)S(1)} %sum_over_prototypes.3), channel_id=1, replica_groups=mesh['dp'=8,'proto'=32] {'proto'}, dimensions={0} | all-to-all | bytes 163840 | tf_op jit(solution)/shard_map/all_to_all | solution.py:317
  92.5 1.3 %sum_over_rows.3 = bf16[8,32,128]{2,1,0:T(8,128)(2,1)S(1)} custom-call(f32[32,1,640]{2,1,0:T(1,128)S(1)} %all_to_all.39.parts_ref, bf16[640,4096]{1,0:T(8,128)(2,1)S(1)} %get-tuple-element.39.exp_ref), custom_call_target="tpu_custom_call" | custom-call | flops 5242880 | bytes 5242880 | tf_op jit(solution)/shard_map/sum_over_rows/pallas_call | solution.py:413
  93.9 11.5 %all_to_all.40.parts_ref = bf16[8,32,128]{2,1,0:T(8,128)(2,1)S(1)} all-to-all(bf16[8,32,128]{2,1,0:T(8,128)(2,1)S(1)} %sum_over_rows.3), channel_id=1, replica_groups=mesh['dp'=8,'proto'=32] {'dp'}, dimensions={0} | all-to-all | bytes 131072 | tf_op jit(solution)/shard_map/all_to_all | solution.py:317
  105.4 1.6 %collective-permute-start.3 = (bf16[8,32,128]{2,1,0:T(8,128)(2,1)S(1)}, bf16[8,32,128]{2,1,0:T(8,128)(2,1)S(1)}, u32[]{:S(2)}, u32[]{:S(2)}) collective-permute-start(bf16[8,32,128]{2,1,0:T(8,128)(2,1)S(1)} %all_to_all.40.parts_ref), channel_id=1, source_target_pairs={{0,1},{1,0},{2,3},{3,2},{4,5},{5,4},{6,7},{7,6},{8,9},{9,8},{10,11... | collective-permute-start | bytes 196616 | tf_op jit(solution)/shard_map/ppermute | solution.py:335
  106.9 0.6 repel_own_core.1
  107.5 0.8 teacher_other_core.1.exp_ref
  108.3 0.0 collective-permute-done.3.parts_ref
  108.4 0.0 copy-start
  108.4 0.6 repel_other_core.1
  108.9 15.6 %all_to_all.41.back_ref = bf16[16,104,128]{2,1,0:T(8,128)(2,1)S(1)} all-to-all(bf16[16,104,128]{2,1,0:T(8,128)(2,1)S(1)} %repel_other_core.1), channel_id=1, replica_groups={{0,2,4,6,8,10,12,14,16,18,20,22,24,26,28,30},{1,3,5,7,9,11,13,15,17,19,..., dimensions={0} | all-to-all | bytes 851968 | tf_op jit(solution)/shard_map/all_to_all | solution.py:317
  124.5 0.0 copy-done
  124.5 0.8 gradients.1
  (1 shorter events, 0.0 us)
Async XLA Ops:
  23.6 5.9 %collective-permute-start = (bf16[16,120,128]{2,1,0:T(8,128)(2,1)S(1)}, bf16[16,120,128]{2,1,0:T(8,128)(2,1)S(1)}, u32[]{:S(2)}, u32[]{:S(2)}) collective-permute-start(bf16[16,120,128]{2,1,0:T(8,128)(2,1)S(1)} %all_to_all.35.own_ref), channel_id=1, source_target_pairs={{0,1},{1,0},{2,3},{3,2},{4,5},{5,4},{6,7},{7,6},{8,9},{9,8},{10,11... | collective-permute-start | bytes 1474568 | tf_op jit(solution)/shard_map/ppermute | solution.py:335
  29.5 9.1 %collective-permute-start.2 = (bf16[4096,256]{1,0:T(8,128)(2,1)S(1)}, bf16[4096,256]{1,0:T(8,128)(2,1)S(1)}, u32[]{:S(2)}, u32[]{:S(2)}) collective-permute-start(bf16[4096,256]{1,0:T(8,128)(2,1)S(1)} %unit_prototypes.1.unit_ref), channel_id=1, source_target_pairs={{0,1},{1,0},{2,3},{3,2},{4,5},{5,4},{6,7},{7,6},{8,9},{9,8},{10,11... | collective-permute-start | bytes 6291464 | tf_op jit(solution)/shard_map/ppermute | solution.py:335
  31.2 10.5 %collective-permute-start.1 = (f32[32,128]{1,0:T(8,128)S(1)}, f32[32,128]{1,0:T(8,128)S(1)}, u32[]{:S(2)}, u32[]{:S(2)}) collective-permute-start(f32[32,128]{1,0:T(8,128)S(1)} %get-tuple-element.32.mine_ref), channel_id=1, source_target_pairs={{0,128},{32,160},{64,192},{96,224},{128,0},{160,32},{192,64},{224,... | collective-permute-start | bytes 49160 | tf_op jit(solution)/shard_map/ppermute | solution.py:373
  105.4 3.0 %collective-permute-start.3 = (bf16[8,32,128]{2,1,0:T(8,128)(2,1)S(1)}, bf16[8,32,128]{2,1,0:T(8,128)(2,1)S(1)}, u32[]{:S(2)}, u32[]{:S(2)}) collective-permute-start(bf16[8,32,128]{2,1,0:T(8,128)(2,1)S(1)} %all_to_all.40.parts_ref), channel_id=1, source_target_pairs={{0,1},{1,0},{2,3},{3,2},{4,5},{5,4},{6,7},{7,6},{8,9},{9,8},{10,11... | collective-permute-start | bytes 196616 | tf_op jit(solution)/shard_map/ppermute | solution.py:335
  108.4 16.2 %copy-start = (bf16[4,10,256]{2,0,1:T(4,128)(2,1)S(1)}, bf16[4,10,256]{2,0,1:T(4,128)(2,1)}, u32[]{:S(2)}) copy-start(bf16[4,10,256]{2,0,1:T(4,128)(2,1)} %param.6) | copy-start | bytes 61444
